TPU v7x, 32 devices: a whole 2x2x4 slice. The times are simulated.
32 devices in a mesh: dom: 2 (over x), shot: 8 (over z, y), space: 2 (over core).
Axes of the slice: x: 2, y: 2, z: 4, core: 2. Of those that a mesh axis runs over, the one named last changes fastest.
Arguments:
- wave_prev: float32 [16, 64, 64, 128], P(('dom', 'shot'), 'space'), parts along dimension 0, may hold values from -13 to 13
- wave_now: float32 [16, 64, 64, 128], P(('dom', 'shot'), 'space'), parts along dimension 0, may hold values from -13 to 13
- velocity_code: int32 [128, 64, 128], P(('dom', 'space')), parts along dimension 0, may hold values from 0 to 255
- perturb: float32 [128, 64, 128], P(('dom', 'space'), None, 'shot'), parts along dimension 0, may hold values from -3 to 3
- gains: float32 [256, 64], P(('dom', 'shot')), parts along dimension 0, may hold values from 0.25 to 4
- wavelet: float32 [16, 4], P(('dom', 'shot')), parts along dimension 0, may hold values from -12 to 12
- source_index: int32 [16], P(('dom', 'shot')), parts along dimension 0, may hold values from 0 to 524287
- receiver_index: int32 [16, 256], P(('dom', 'shot')), parts along dimension 0, may hold values from 0 to 524287
- absorb_width: int32 [12], P('dom'), parts along dimension 0, may hold values from 4 to 20
Outputs:
- filtered: float32 [128, 64, 128], P(('dom', 'space'), None, 'shot'), parts along dimension 0
- born_field: float32 [16, 64, 64, 128], P(('dom', 'shot'), 'space'), parts along dimension 0
- traces: float32 [16, 2, 256], P(('dom', 'shot')), parts along dimension 0
There are 2 independent parts, one for each index of `dom`. A program takes and returns all parts, laid end to end along the dimension named above; each array names one. Nothing has to cross between parts.
Inputs may be any that keep to these rules, and one draw needn't show every extreme that they name: `absorb_width`: entries are the widths at the low and high end of the first, second and third dimension, in that order. `source_index`: flat row-major cell indices of the whole window. `receiver_index`: flat row-major cell indices of the whole window.
All inputs are finite; a program needn't handle non-finite values.
Results may differ from a plain program's by a relative error of at most 0.0003.
Values sent between devices are 32-bit elements; how exact they have to be, the bound alone decides.
A program may use at most 64 MiB of HBM per device.

v0:
```python
import math

import jax
import jax.numpy as jnp
from jax import lax
from jax.sharding import PartitionSpec as P

STEPS_A = 2
STEPS_B = 2


STENCIL = (-205.0 / 72.0, 8.0 / 5.0, -1.0 / 5.0, 8.0 / 315.0, -1.0 / 560.0)
damp_peak = 0.5
eps = 1e-05


def with_halo(x, sides, width):
    for axis, dim in sides:
        size, length = (lax.axis_size(axis), x.shape[dim])
        up = [(i, (i + 1) % size) for i in range(size - 1)]
        down = [(j, i) for i, j in up]
        last = lax.slice_in_dim(x, length - width, length, axis=dim)
        first = lax.slice_in_dim(x, 0, width, axis=dim)
        before = lax.ppermute(last, axis, up)
        after = lax.ppermute(first, axis, down)
        x = jnp.concatenate([before, x, after], axis=dim)
    return x


def coefficient(levels):
    speed = 1500.0 + 15.0 * levels.astype(jnp.float32)
    ratio = 0.45 * speed / 5325.0
    return ratio * ratio


def ramp(position, count, lower, upper):
    low_part = jnp.maximum(lower - position, 0.0) / lower
    high_part = jnp.maximum(upper - (count - 1.0 - position), 0.0) / upper
    return low_part * low_part + high_part * high_part


def damping(widths, positions, count_x, count_y, count_z):
    edges = widths.astype(jnp.float32)
    along_x = ramp(positions, count_x, edges[0], edges[1])
    along_y = ramp(jnp.arange(count_y, dtype=jnp.float32), count_y, edges[2], edges[3])
    along_z = ramp(jnp.arange(count_z, dtype=jnp.float32), count_z, edges[4], edges[5])
    return damp_peak * (along_x[:, None, None] + along_y[None, :, None] + along_z[None, None, :])


def widen(field):
    lead = [(0, 0)] * (field.ndim - 2)
    return jnp.pad(field, lead + [(4, 4), (4, 4)])


def laplace(padded):
    width_x = padded.shape[-3] - 8
    width_y = padded.shape[-2] - 8
    width_z = padded.shape[-1] - 8

    def part(move_x, move_y, move_z):
        return padded[
            ...,
            4 + move_x : 4 + move_x + width_x,
            4 + move_y : 4 + move_y + width_y,
            4 + move_z : 4 + move_z + width_z,
        ]

    total = 3.0 * STENCIL[0] * part(0, 0, 0)
    for reach in range(1, 5):
        beside_all = (
            part(reach, 0, 0)
            + part(-reach, 0, 0)
            + part(0, reach, 0)
            + part(0, -reach, 0)
            + part(0, 0, reach)
            + part(0, 0, -reach)
        )
        total = total + STENCIL[reach] * beside_all
    return total


def lateral_filter(field, table):
    count = field.shape[1]
    index = jnp.arange(count)
    phase = index[:, None] * index[None, :] % count
    angle = 2.0 * math.pi / count * phase.astype(jnp.float32)
    cosine = jnp.cos(angle)
    sine = jnp.sin(angle)
    real_part = jnp.einsum("xyz,yk->xzk", field, cosine, precision=lax.Precision.HIGHEST)
    imag_part = jnp.einsum("xyz,yk->xzk", field, sine, precision=lax.Precision.HIGHEST)
    weight = table[None, :, :]
    back = jnp.einsum("xzk,yk->xyz", real_part * weight, cosine, precision=lax.Precision.HIGHEST)
    back = back + jnp.einsum(
        "xzk,yk->xyz", imag_part * weight, sine, precision=lax.Precision.HIGHEST
    )
    return back / count


def body(
    wave_prev,
    wave_now,
    velocity_code,
    perturb,
    gains,
    wavelet,
    source_index,
    receiver_index,
    absorb_width,
):
    shots, span_x, span_y, span_z = wave_now.shape
    start_x = lax.axis_index("space") * span_x
    total_x = span_x * lax.axis_size("space")
    speed_term = coefficient(velocity_code)
    positions = start_x.astype(jnp.float32) + jnp.arange(span_x, dtype=jnp.float32)
    absorber = damping(absorb_width, positions, total_x, span_y, span_z)
    term_flat = speed_term.reshape(-1)
    cells = span_x * span_y * span_z
    offset = start_x * span_y * span_z
    rows = jnp.arange(shots)
    source_local = source_index - offset
    source_owned = (source_local >= 0) & (source_local < cells)
    source_safe = jnp.clip(source_local, 0, cells - 1)
    source_gain = jnp.where(source_owned, term_flat[source_safe], 0.0)
    model = lax.all_gather(perturb, "shot", axis=2, tiled=True)

    def inject(field, moment):
        flat = field.reshape(shots, -1)
        flat = flat.at[rows, source_safe].add(source_gain * wavelet[:, moment])
        return flat.reshape(field.shape)

    def advance(current, prior, born, field_model, moment, first):
        if first:
            padded = widen(with_halo(current, (("space", 1),), 4))
        else:
            both = widen(with_halo(jnp.stack([current, born]), (("space", 2),), 4))
            padded = both[0]
            born_padded = both[1]
        drive = speed_term * laplace(padded)
        later = inject(2.0 * current - prior + drive - absorber * (current - prior), moment)
        if first:
            born_later = field_model * drive
        else:
            born_later = (
                2.0 * born
                + speed_term * laplace(born_padded)
                - absorber * born
                + field_model * drive
            )
        return (later, born_later, drive)

    current, prior = (wave_now, wave_prev)
    born = None
    image = jnp.zeros((span_x, span_y, span_z), jnp.float32)
    light = jnp.zeros((span_x, span_y, span_z), jnp.float32)
    for moment in range(STEPS_A):
        later, born_later, drive = advance(current, prior, born, model, moment, moment == 0)
        image = image + jnp.sum(drive * born_later, axis=0)
        light = light + jnp.sum(drive * drive, axis=0)
        prior, current = (current, later)
        born = born_later
    planes = gains.shape[0]
    image_all, light_all = lax.psum((image, light), "shot")
    table_all = lax.all_gather(gains, "shot", axis=0, tiled=True)
    new_model = lateral_filter(image_all / (light_all + eps), table_all)
    filtered = lax.dynamic_slice_in_dim(new_model, lax.axis_index("shot") * planes, planes, 2)
    receiver_local = receiver_index - offset
    receiver_owned = (receiver_local >= 0) & (receiver_local < cells)
    receiver_safe = jnp.clip(receiver_local, 0, cells - 1)
    born = None
    records = []
    for moment in range(STEPS_B):
        later, born_later, drive = advance(
            current, prior, born, new_model, STEPS_A + moment, moment == 0
        )
        sample = jnp.take_along_axis(born_later.reshape(shots, -1), receiver_safe, axis=1)
        records.append(jnp.where(receiver_owned, sample, 0.0))
        prior, current = (current, later)
        born = born_later
    traces = lax.psum(jnp.stack(records, axis=1), "space")
    return (filtered, born, traces)


def solution(mesh):
    in_specs = (
        P(("dom", "shot"), "space", None, None),
        P(("dom", "shot"), "space", None, None),
        P(("dom", "space"), None, None),
        P(("dom", "space"), None, "shot"),
        P(("dom", "shot"), None),
        P(("dom", "shot"), None),
        P(("dom", "shot")),
        P(("dom", "shot"), None),
        P("dom"),
    )
    out_specs = (
        P(("dom", "space"), None, "shot"),
        P(("dom", "shot"), "space", None, None),
        P(("dom", "shot"), None, None),
    )
    return jax.shard_map(body, mesh=mesh, in_specs=in_specs, out_specs=out_specs, check_vma=False)
```

profile of v0, /device:TPU:0, one launch (start us, length us, event | category | flops | bytes accessed | tf_op | source)
XLA Modules:
  0.0 278.1 jit_solution(2789940103628602469)
XLA Ops:
  7.2 1.7 fusion.136
  9.0 2.4 collective-permute-start.1
  12.6 1.7 copy.18
  27.0 7.3 %multiply_subtract_fusion.2 = (f32[1,32,64,128]{3,2,1,0:T(8,128)S(1)}, f32[1,32,64,128]{3,2,1,0:T(8,128)}) fusion(f32[1,32,64,128]{3,2,1,0:T(8,128)} %param.18, f32[1,32,64,128]{3,2,1,0:T(8,128)} %param.17, f32[128]{0:T(128)S(1)} %fusion.117, f32[32,64]{1,0:T(8,128)S(1)} %broadcast_add_fusion, f32[1,40,72,136]{3,2,1,0:T(8,128)S(1)} %select_maximum_fusion.8, ...), kind=kLoop, calls=%fused_computation.250 | loop fusion | flops 11272192 | bytes 30417408 | tf_op jit(solution)/shard_map/sub | solution.py:139
  36.9 29.7 %all-gather.2.cloned.1.call-done = f32[32,64,128]{1,0,2:T(8,128)} async-done(((f32[32,64,16]{1,0,2:T(8,128)}), f32[32,64,128]{1,0,2:T(8,128)}) %all-gather.2.cloned.1.call-update) | async-done | bytes 1048592 | tf_op jit(solution)/shard_map/all_gather | solution.py:124
  66.7 3.7 %copy.19 = f32[32,64,128]{2,1,0:T(8,128)} copy(f32[32,64,128]{1,0,2:T(8,128)} %all-gather.2.cloned.1.call-done) | data formatting | bytes 2097152 | tf_op jit(solution)/shard_map/all_gather | solution.py:124
  74.6 1.9 collective-permute-done.3
  76.5 4.7 %select_maximum_fusion.3 = f32[2,1,40,72,136]{4,3,2,1,0:T(8,128)S(1)} fusion(f32[2,1,4,64,128]{4,3,2,1,0:T(8,128)S(1)} %collective-permute-done.3, f32[2,1,4,64,128]{4,3,2,1,0:T(8,128)S(1)} %collective-permute-done.2, f32[1,1,32,64,128]{4,3,2,1,0:T(8,128)S(1)} %fusion.93, f32[1,1,32,64,128]{4,3,2,1,0:T(8,128)S(1)} %bitcast.94), kind=kLoop, calls=%fused_computation.9 | loop fusion | flops 14100480 | bytes 5754880 | tf_op jit(solution)/shard_map/concatenate | solution.py:26
  82.5 8.2 %multiply_subtract_fusion.1 = (f32[1,32,64,128]{3,2,1,0:T(8,128)}, f32[1,32,64,128]{3,2,1,0:T(8,128)S(1)}) fusion(f32[1,32,64,128]{3,2,1,0:T(8,128)S(1)} %bitcast.95, f32[1,32,64,128]{3,2,1,0:T(8,128)S(1)} %copy-done.4, f32[128]{0:T(128)S(1)} %copy-done.12, f32[32,64]{1,0:T(8,128)S(1)} %broadcast_add_fusion, f32[1,40,72,136]{3,2,1,0:T(8,128)S(1)} %get-tuple-element.71, ...), kind=kLoop, calls=%fused_computation.246 | loop fusion | flops 11272192 | bytes 31465984 | tf_op jit(solution)/shard_map/sub | solution.py:139
  92.2 8.2 %fusion.68 = f32[32,64,128]{2,1,0:T(8,128)} fusion(f32[1,32,64,128]{3,2,1,0:T(8,128)S(1)} %get-tuple-element.65, f32[1,40,72,136]{3,2,1,0:T(8,128)S(1)} %get-tuple-element.70, f32[32,64,128]{2,1,0:T(8,128)S(1)} %copy-done.9, f32[1,32,64,128]{3,2,1,0:T(8,128)S(1)} %copy-done.6, f32[128]{0:T(128)S(1)} %copy-done.12, f32[32,64]{1,0:T(8,128)S(1)} %broadcast_add_fusion, ...), kind=kLoop, calls=%fused_computation.156 | loop fusion | flops 12320768 | bytes 31465984 | tf_op jit(solution)/shard_map/add | solution.py:157
  108.1 3.0 %collective-permute-start.5 = (f32[1,4,64,128]{3,2,1,0:T(8,128)S(1)}, f32[1,4,64,128]{3,2,1,0:T(8,128)S(1)}, u32[]{:S(2)}, u32[]{:S(2)}) collective-permute-start(f32[1,4,64,128]{3,2,1,0:T(8,128)S(1)} %get-tuple-element.76), channel_id=1, source_target_pairs={{0,1},{2,3},{4,5},{6,7},{8,9},{10,11},{12,13},{14,15},{16,17},{18,... | collective-permute-start | bytes 393224 | tf_op jit(solution)/shard_map/ppermute | solution.py:24
  111.8 31.3 %all_gather.7 = f32[128,64]{1,0:T(8,128)S(1)} all-gather(f32[16,64]{1,0:T(8,128)S(1)} %copy-done.14), channel_id=1, replica_groups=mesh['dom'=2,'shot'=8,'space'=2] {'shot'}, dimensions={0}, use_global_device_ids=true | all-gather | bytes 36864 | tf_op jit(solution)/shard_map/all_gather | solution.py:163
  143.1 2.1 select_maximum_fusion.6
  145.2 10.9 %multiply_subtract_fusion = (f32[1,32,64,128]{3,2,1,0:T(8,128)}, f32[1,32,64,128]{3,2,1,0:T(8,128)}) fusion(f32[1,32,64,128]{3,2,1,0:T(8,128)} %bitcast.104, f32[1,32,64,128]{3,2,1,0:T(8,128)} %bitcast.96, f32[128]{0:T(128)S(1)} %copy-done.12, f32[32,64]{1,0:T(8,128)S(1)} %broadcast_add_fusion, f32[1,40,72,136]{3,2,1,0:T(8,128)S(1)} %select_maximum_fusion.6, ...), kind=kLoop, calls=%fused_computation.245 | loop fusion | flops 13369344 | bytes 22290944 | tf_op jit(solution)/shard_map/sub | solution.py:139
  160.7 41.5 %all-reduce.7.cloned.1.call-done = (f32[32,64,128]{2,1,0:T(8,128)}, f32[32,64,128]{2,1,0:T(8,128)}) async-done(((f32[32,64,128]{2,1,0:T(8,128)}, f32[32,64,128]{2,1,0:T(8,128)}), (f32[32,64,128]{2,1,0:T(8,128)}, f32[32,64,128]{2,1,0:T(8,128)})) %all-reduce.7.cloned.1.call-update) | async-done | bytes 2097168 | tf_op jit(solution)/shard_map/psum | solution.py:162
  202.1 3.0 %convolution_multiply_fusion = f32[32,128,64]{1,2,0:T(8,128)S(1)} fusion(f32[128,64]{0,1:T(8,128)S(1)} %copy.21, f32[32,64,128]{2,1,0:T(8,128)} %get-tuple-element.60, f32[32,64,128]{2,1,0:T(8,128)} %get-tuple-element.61), kind=kOutput, calls=%fused_computation.38 | convolution fusion | flops 202170368 | bytes 3178496 | tf_op jit(solution)/shard_map/xyz,yk->xzk/dot_general | solution.py:90
  210.2 1.5 collective-permute-start.6
  214.4 2.2 copy.23
  216.6 1.7 gather_fusion
  218.4 4.5 %select_maximum_fusion = f32[2,1,40,72,136]{4,3,2,1,0:T(8,128)S(1)} fusion(f32[2,1,4,64,128]{4,3,2,1,0:T(8,128)} %collective-permute-done.7, f32[2,1,4,64,128]{4,3,2,1,0:T(8,128)S(1)} %collective-permute-done.6, f32[1,1,32,64,128]{4,3,2,1,0:T(8,128)S(1)} %bitcast.99, f32[1,1,32,64,128]{4,3,2,1,0:T(8,128)S(1)} %bitcast.108), kind=kLoop, calls=%fused_computation.6 | loop fusion | flops 14100480 | bytes 5754880 | tf_op jit(solution)/shard_map/concatenate | solution.py:26
  222.9 2.1 slice_bitcast_fusion.1
  225.0 35.2 %fusion.40 = f32[1,32,64,128]{3,2,1,0:T(8,128)} fusion(f32[1,40,72,136]{3,2,1,0:T(8,128)} %get-tuple-element.69, f32[1,40,72,136]{3,2,1,0:T(8,128)S(1)} %get-tuple-element.68, f32[64,32,128]{2,0,1:T(8,128)} %copy-done.5, f32[1,32,64,128]{3,2,1,0:T(8,128)} %copy-done.2, f32[128]{0:T(128)S(1)} %copy-done.13, f32[32,64]{1,0:T(8,128)S(1)} %broadcast_add_fusion, ...), kind=kLoop, calls=%fused_computation.80 | loop fusion | flops 19136512 | bytes 56631808 | tf_op jit(solution)/shard_map/add | solution.py:144
  260.2 6.2 %gather_fusion.1 = f32[256]{0:T(256)S(1)} fusion(f32[262144]{0:T(1024)} %bitcast.109, s32[1024]{0:T(1024)S(1)} %pad_clamp_fusion), kind=kCustom, calls=%fused_computation.1.clone | custom fusion | bytes 3072 | tf_op jit(solution)/shard_map/jit(take_along_axis)/gather | solution.py:175
  266.5 4.8 %psum.23 = f32[1,2,256]{2,1,0:T(2,128)} all-reduce(f32[1,2,256]{2,1,0:T(2,128)S(1)} %pad_maximum_fusion.6), channel_id=1, replica_groups=mesh['dom'=2,'shot'=8,'space'=2] {'space'}, use_global_device_ids=true, to_apply=%region_3.5 | all-reduce | flops 512 | bytes 4096 | tf_op jit(solution)/shard_map/psum | solution.py:179
  (90 shorter events, 34.8 us)
Async XLA Ops:
  7.2 17.7 %copy-start.3 = (f32[1,32,64,128]{3,2,1,0:T(8,128)S(1)}, f32[1,32,64,128]{3,2,1,0:T(8,128)}, u32[]{:S(2)}) copy-start(f32[1,32,64,128]{3,2,1,0:T(8,128)} %param.18) | copy-start | bytes 3145732
  7.2 12.5 %copy-start.15 = (f32[1,4]{1,0:T(1,128)S(1)}, f32[1,4]{1,0:T(1,128)}, u32[]{:S(2)}) copy-start(f32[1,4]{1,0:T(1,128)} %param.22) | copy-start | bytes 52
  7.2 59.5 %all-gather.2.cloned.1.call-start = ((), (), s32[]{:S(2)}) async-start(), calls=%async_computation | async-start | bytes 2359296 | tf_op jit(solution)/shard_map/all_gather | solution.py:124
  9.0 15.8 %collective-permute-start.1 = (f32[1,4,64,128]{3,2,1,0:T(8,128)S(1)}, f32[1,4,64,128]{3,2,1,0:T(8,128)S(1)}, u32[]{:S(2)}, u32[]{:S(2)}) collective-permute-start(f32[1,4,64,128]{3,2,1,0:T(8,128)S(1)} %get-tuple-element.80), channel_id=1, source_target_pairs={{0,1},{2,3},{4,5},{6,7},{8,9},{10,11},{12,13},{14,15},{16,17},{18,... | collective-permute-start | bytes 393224 | tf_op jit(solution)/shard_map/ppermute | solution.py:24
  11.3 13.8 %collective-permute-start = (f32[1,4,64,128]{3,2,1,0:T(8,128)}, f32[1,4,64,128]{3,2,1,0:T(8,128)S(1)}, u32[]{:S(2)}, u32[]{:S(2)}) collective-permute-start(f32[1,4,64,128]{3,2,1,0:T(8,128)} %get-tuple-element.81), channel_id=1, source_target_pairs={{1,0},{3,2},{5,4},{7,6},{9,8},{11,10},{13,12},{15,14},{17,16},{19,... | collective-permute-start | bytes 393224 | tf_op jit(solution)/shard_map/ppermute | solution.py:25
  14.4 187.8 %all-reduce.7.cloned.1.call-start = ((), (), s32[]{:S(2)}) async-start(), calls=%async_computation.1 | async-start | bytes 4194304 | tf_op jit(solution)/shard_map/psum | solution.py:162
  24.8 2.2 copy-start.11
  25.1 1.9 copy-start
  34.3 36.0 %copy-start.6 = (f32[1,32,64,128]{3,2,1,0:T(8,128)S(1)}, f32[1,32,64,128]{3,2,1,0:T(8,128)}, u32[]{:S(2)}) copy-start(f32[1,32,64,128]{3,2,1,0:T(8,128)} %get-tuple-element.67) | copy-start | bytes 3145732
  36.9 44.7 %copy-start.1 = (f32[1,262144]{1,0:T(1,128)}, f32[1,262144]{1,0:T(1,128)S(1)}, u32[]{:S(2)}) copy-start(f32[1,262144]{1,0:T(1,128)S(1)} %scatter-add.10) | copy-start | bytes 3145732
  71.8 2.8 %collective-permute-start.2 = (f32[2,1,4,64,128]{4,3,2,1,0:T(8,128)S(1)}, f32[2,1,4,64,128]{4,3,2,1,0:T(8,128)S(1)}, u32[]{:S(2)}, u32[]{:S(2)}) collective-permute-start(f32[2,1,4,64,128]{4,3,2,1,0:T(8,128)S(1)} %get-tuple-element.74), channel_id=1, source_target_pairs={{0,1},{2,3},{4,5},{6,7},{8,9},{10,11},{12,13},{14,15},{16,17},{18,... | collective-permute-start | bytes 786440 | tf_op jit(solution)/shard_map/ppermute | solution.py:24
  73.1 3.4 %collective-permute-start.3 = (f32[2,1,4,64,128]{4,3,2,1,0:T(8,128)S(1)}, f32[2,1,4,64,128]{4,3,2,1,0:T(8,128)S(1)}, u32[]{:S(2)}, u32[]{:S(2)}) collective-permute-start(f32[2,1,4,64,128]{4,3,2,1,0:T(8,128)S(1)} %get-tuple-element.75), channel_id=1, source_target_pairs={{1,0},{3,2},{5,4},{7,6},{9,8},{11,10},{13,12},{15,14},{17,16},{19,... | collective-permute-start | bytes 786440 | tf_op jit(solution)/shard_map/ppermute | solution.py:25
  92.2 19.5 %copy-start.14 = (f32[16,64]{1,0:T(8,128)S(1)}, f32[16,64]{1,0:T(8,128)}, u32[]{:S(2)}) copy-start(f32[16,64]{1,0:T(8,128)} %param.21) | copy-start | bytes 12292
  106.8 36.3 %collective-permute-start.4 = (f32[1,4,64,128]{3,2,1,0:T(8,128)S(1)}, f32[1,4,64,128]{3,2,1,0:T(8,128)S(1)}, u32[]{:S(2)}, u32[]{:S(2)}) collective-permute-start(f32[1,4,64,128]{3,2,1,0:T(8,128)S(1)} %get-tuple-element.77), channel_id=1, source_target_pairs={{1,0},{3,2},{5,4},{7,6},{9,8},{11,10},{13,12},{15,14},{17,16},{19,... | collective-permute-start | bytes 393224 | tf_op jit(solution)/shard_map/ppermute | solution.py:25
  108.1 35.0 %collective-permute-start.5 = (f32[1,4,64,128]{3,2,1,0:T(8,128)S(1)}, f32[1,4,64,128]{3,2,1,0:T(8,128)S(1)}, u32[]{:S(2)}, u32[]{:S(2)}) collective-permute-start(f32[1,4,64,128]{3,2,1,0:T(8,128)S(1)} %get-tuple-element.76), channel_id=1, source_target_pairs={{0,1},{2,3},{4,5},{6,7},{8,9},{10,11},{12,13},{14,15},{16,17},{18,... | collective-permute-start | bytes 393224 | tf_op jit(solution)/shard_map/ppermute | solution.py:24
  202.1 3.0 %copy-start.17 = (f32[32,64,128]{2,1,0:T(8,128)S(1)}, f32[32,64,128]{2,1,0:T(8,128)}, u32[]{:S(2)}) copy-start(f32[32,64,128]{2,1,0:T(8,128)} %get-tuple-element.60) | copy-start | bytes 3145732
  202.1 3.0 %copy-start.18 = (f32[32,64,128]{2,1,0:T(8,128)S(1)}, f32[32,64,128]{2,1,0:T(8,128)}, u32[]{:S(2)}) copy-start(f32[32,64,128]{2,1,0:T(8,128)} %get-tuple-element.61) | copy-start | bytes 3145732
  206.5 2.4 copy-start.10
  208.9 5.4 %copy-start.5 = (f32[64,32,128]{2,0,1:T(8,128)}, f32[64,32,128]{2,0,1:T(8,128)S(1)}, u32[]{:S(2)}) copy-start(f32[64,32,128]{2,0,1:T(8,128)S(1)} %fusion.6) | copy-start | bytes 3145732
  208.9 4.1 %copy-start.16 = (s32[1,256]{1,0:T(1,128)S(1)}, s32[1,256]{1,0:T(1,128)}, u32[]{:S(2)}) copy-start(s32[1,256]{1,0:T(1,128)} %param.24) | copy-start | bytes 3076
  209.1 9.2 %copy-start.2 = (f32[1,32,64,128]{3,2,1,0:T(8,128)}, f32[1,32,64,128]{3,2,1,0:T(8,128)S(1)}, u32[]{:S(2)}) copy-start(f32[1,32,64,128]{3,2,1,0:T(8,128)S(1)} %bitcast_multiply_fusion) | copy-start | bytes 3145732
  210.2 8.2 %collective-permute-start.6 = (f32[2,1,4,64,128]{4,3,2,1,0:T(8,128)}, f32[2,1,4,64,128]{4,3,2,1,0:T(8,128)S(1)}, u32[]{:S(2)}, u32[]{:S(2)}) collective-permute-start(f32[2,1,4,64,128]{4,3,2,1,0:T(8,128)} %get-tuple-element.72), channel_id=1, source_target_pairs={{0,1},{2,3},{4,5},{6,7},{8,9},{10,11},{12,13},{14,15},{16,17},{18,... | collective-permute-start | bytes 786440 | tf_op jit(solution)/shard_map/ppermute | solution.py:24
  211.7 6.7 %collective-permute-start.7 = (f32[2,1,4,64,128]{4,3,2,1,0:T(8,128)}, f32[2,1,4,64,128]{4,3,2,1,0:T(8,128)}, u32[]{:S(2)}, u32[]{:S(2)}) collective-permute-start(f32[2,1,4,64,128]{4,3,2,1,0:T(8,128)} %get-tuple-element.73), channel_id=1, source_target_pairs={{1,0},{3,2},{5,4},{7,6},{9,8},{11,10},{13,12},{15,14},{17,16},{19,... | collective-permute-start | bytes 786440 | tf_op jit(solution)/shard_map/ppermute | solution.py:25
  222.9 2.1 copy-start.13
  (5 other events, 6.4 us)
Sparse Core Ops, SparseCore 0:
  14.5 52.1 all-gather.1
  100.6 101.5 all-reduce.6
where the time goes:
time: 279 us; the launch traced here: 278 us
  other arithmetic  95.6 us (34%)
  waiting for transfers between devices  73.2 us (26%)
  blocking collectives  36.1 us (13%)
  local copies, waits for them, and re-layouts  29.2 us (10%)
  between operations  23.6 us (8%)
  starting transfers between devices  13.6 us (5%)
  matrix products  6.7 us (2%)
    psum x1, waiting for transfers between devices, body(): image_all, light_all = lax.psum((image, light), 'shot')  41.5 us
    add x1, other arithmetic, advance(): 2.0 * born + speed_term * laplace(born_padded) - absorber * born  35.2 us
    all_gather x1, blocking collectives, body(): table_all = lax.all_gather(gains, 'shot', axis=0, tiled=True)  31.3 us
    all_gather x1, waiting for transfers between devices, body(): model = lax.all_gather(perturb, 'shot', axis=2, tiled=True)  29.7 us
    sub x3, other arithmetic, advance(): 2.0 * current - prior + drive - absorber * (current - prior)  26.4 us
    concatenate x4, other arithmetic, with_halo(): x = jnp.concatenate([before, x, after], axis=dim)  12.2 us
    ppermute x4, starting transfers between devices, with_halo(): before = lax.ppermute(last, axis, up)  8.22 us
    add x1, other arithmetic, body(): image = image + jnp.sum(drive * born_later, axis=0)  8.2 us
  transfers between devices with their start and end apart: 10, of which 3 were waited for; matrix products, arithmetic and copies ran while one was open for 16% of the time, Pallas kernels for 0%

commit v1 on v0

--- a/solution.py
+++ b/solution.py
@@ -2,7 +2,11 @@
 
 import jax
 import jax.numpy as jnp
+import ml_dtypes
+import numpy as np
 from jax import lax
+from jax.experimental import pallas as pl
+from jax.experimental.pallas import tpu as pltpu
 from jax.sharding import PartitionSpec as P
 
 STEPS_A = 2
@@ -180,6 +184,516 @@
     return (filtered, born, traces)
 
 
+XB = 8
+MESH = pl.DeviceIdType.MESH
+
+
+def swap_groups(tiles, width):
+    lane = lax.broadcasted_iota(jnp.int32, tiles[0].shape, 1) // width
+    tiles = list(tiles)
+    span = width * len(tiles)
+    for bit in (1, 2, 4):
+        upper = (lane & bit) != 0
+        for i in range(len(tiles)):
+            if i & bit:
+                continue
+            a, b = tiles[i], tiles[i | bit]
+            tiles[i] = jnp.where(upper, pltpu.roll(b, width * bit, 1), a)
+            tiles[i | bit] = jnp.where(upper, b, pltpu.roll(a, span - width * bit, 1))
+    return tiles
+
+
+def window_kernel(
+    prev_ref, now_ref, code_ref, pert_ref, gain_ref, cos_ref, band_ref,
+    wavelet_ref, source_ref, receiver_ref, width_ref,
+    filt_ref, born_ref, trace_ref,
+    W, D, B, M, C, A, PAD, BASE, G, LP, LY, LU, LD, IP, IY, IU, ID, H, ROWS, TR,
+    in_sem, halo_send, halo_recv, tr_send, tr_recv,
+    g_send, g_recv, rs_send, rs_recv,
+):
+    core = lax.axis_index("space")
+    shot = lax.axis_index("shot")
+    y = lax.rem(shot, 2)
+    z = shot // 2
+    nx, ny, nz = code_ref.shape
+    width = pert_ref.shape[2]
+    groups = nz // width
+    start_x = core * nx
+    other = {"space": 1 - core}
+    beside = {"shot": 2 * z + 1 - y}
+    above = {"shot": shot + 2}
+    below = {"shot": shot - 2}
+
+    load = pltpu.make_async_copy(now_ref, W.at[0, pl.ds(4, nx), pl.ds(8, ny)], in_sem)
+    load.start()
+
+    barrier = pltpu.get_barrier_semaphore()
+    pl.semaphore_signal(barrier, inc=1, device_id=other, device_id_type=MESH)
+    pl.semaphore_signal(barrier, inc=1, device_id=beside, device_id_type=MESH)
+
+    @pl.when(z < 3)
+    def _():
+        pl.semaphore_signal(barrier, inc=1, device_id=above, device_id_type=MESH)
+
+    @pl.when(z > 0)
+    def _():
+        pl.semaphore_signal(barrier, inc=1, device_id=below, device_id_type=MESH)
+
+    lane_group = lax.broadcasted_iota(jnp.int32, (8, nz), 1) // width
+
+    @pl.loop(0, nx)
+    def _(i):
+        PAD[:, 0:width] = pert_ref[i]
+        tile = PAD[0:8, :]
+        for g in range(1, groups):
+            tile = jnp.where(lane_group == g, pltpu.roll(PAD[8 * g : 8 * g + 8, :], width * g, 1), tile)
+        G[0, shot, i] = tile
+
+    @pl.when((z > 0) & (z < 3))
+    def _():
+        pl.semaphore_wait(barrier, 4)
+
+    @pl.when((z == 0) | (z == 3))
+    def _():
+        pl.semaphore_wait(barrier, 3)
+
+    def copy(src, dst, send, recv, device):
+        return pltpu.make_async_remote_copy(
+            src_ref=src, dst_ref=dst, send_sem=send, recv_sem=recv, device_id=device, device_id_type=MESH
+        )
+
+    def gather_copy(n, way, at, device):
+        slot = 2 * at + y
+        return copy(G.at[n, slot], G.at[n, slot], g_send.at[n, way, at], g_recv.at[n, slot], device)
+
+    def gather_wait(n, slot):
+        copy(G.at[n, slot], G.at[n, slot], g_send.at[n, 0, 0], g_recv.at[n, slot], beside).wait_recv()
+
+    def gather_start(n):
+        @pl.when(z < 3)
+        def _():
+            gather_copy(n, 1, z, above).start()
+
+        @pl.when(z > 0)
+        def _():
+            gather_copy(n, 2, z, below).start()
+
+        gather_copy(n, 0, z, beside).start()
+
+    def gather_forward(n, d):
+        @pl.when(z - d >= 0)
+        def _():
+            gather_wait(n, 2 * (z - d) + y)
+
+            @pl.when(z < 3)
+            def _():
+                gather_copy(n, 1, z - d, above).start()
+
+            gather_copy(n, 0, z - d, beside).start()
+
+        @pl.when(z + d <= 3)
+        def _():
+            gather_wait(n, 2 * (z + d) + y)
+
+            @pl.when(z > 0)
+            def _():
+                gather_copy(n, 2, z + d, below).start()
+
+            gather_copy(n, 0, z + d, beside).start()
+
+    def gather_end(n):
+        for at in range(4):
+            gather_wait(n, 2 * at + 1 - y)
+
+    def gather_drain(n):
+        for at in range(4):
+            gather_copy(n, 0, at, beside).wait_send()
+
+            @pl.when((z < 3) & (at <= z))
+            def _():
+                gather_copy(n, 1, at, above).wait_send()
+
+            @pl.when((z > 0) & (at >= z))
+            def _():
+                gather_copy(n, 2, at, below).wait_send()
+
+    sums = ((LP, LY, LU, LD), (IP, IY, IU, ID))
+
+    def pair_copy(n, at):
+        P_, Y_, _, _ = sums[n]
+        return copy(P_.at[2 * at + 1 - y], Y_.at[at], rs_send.at[n, 0, at], rs_recv.at[n, 0, at], beside)
+
+    def up_copy(n, at):
+        P_, _, U_, _ = sums[n]
+        return copy(P_.at[2 * at + y], U_.at[at], rs_send.at[n, 1, at], rs_recv.at[n, 1, at], above)
+
+    def down_copy(n, at):
+        P_, _, _, D_ = sums[n]
+        return copy(P_.at[2 * at + y], D_.at[at], rs_send.at[n, 2, at], rs_recv.at[n, 2, at], below)
+
+    def pair_start(n):
+        for d in (3, 2, 1):
+            @pl.when(z + d <= 3)
+            def _():
+                pair_copy(n, z + d).start()
+
+            @pl.when(z - d >= 0)
+            def _():
+                pair_copy(n, z - d).start()
+
+        pair_copy(n, z).start()
+
+    def sum_line(n):
+        P_, Y_, U_, D_ = sums[n]
+        for d in (3, 2, 1):
+            @pl.when(z + d <= 3)
+            def _():
+                at = z + d
+                pair_copy(n, at).wait_recv()
+                P_[2 * at + y] = P_[2 * at + y] + Y_[at]
+
+                @pl.when(z > 0)
+                def _():
+                    up_copy(n, at).wait_recv()
+                    P_[2 * at + y] = P_[2 * at + y] + U_[at]
+
+                up_copy(n, at).start()
+
+            @pl.when(z - d >= 0)
+            def _():
+                at = z - d
+                pair_copy(n, at).wait_recv()
+                P_[2 * at + y] = P_[2 * at + y] + Y_[at]
+
+                @pl.when(z < 3)
+                def _():
+                    down_copy(n, at).wait_recv()
+                    P_[2 * at + y] = P_[2 * at + y] + D_[at]
+
+                down_copy(n, at).start()
+
+    def sum_own(n):
+        P_, Y_, U_, D_ = sums[n]
+        pair_copy(n, z).wait_recv()
+        P_[shot] = P_[shot] + Y_[z]
+
+        @pl.when(z > 0)
+        def _():
+            up_copy(n, z).wait_recv()
+            P_[shot] = P_[shot] + U_[z]
+
+        @pl.when(z < 3)
+        def _():
+            down_copy(n, z).wait_recv()
+            P_[shot] = P_[shot] + D_[z]
+
+    def sum_drain(n):
+        for at in range(4):
+            pair_copy(n, at).wait_send()
+
+            @pl.when(at > z)
+            def _():
+                up_copy(n, at).wait_send()
+
+            @pl.when(at < z)
+            def _():
+                down_copy(n, at).wait_send()
+
+    fields = [W.at[0], W.at[1], W.at[2], W.at[3], B.at[0], B.at[1]]
+
+    def halo(n):
+        field = fields[n]
+        return copy(
+            field.at[pl.ds(4 + (nx - 4) * (1 - core), 4), pl.ds(8, ny)],
+            field.at[pl.ds((nx + 4) * core, 4), pl.ds(8, ny)],
+            halo_send.at[n],
+            halo_recv.at[n],
+            other,
+        )
+
+    gather_start(0)
+    load.wait()
+    halo(0).start()
+
+    edges = [jnp.full((ny, nz), width_ref[i].astype(jnp.float32)) for i in range(6)]
+
+    def ramp_at(position, count, lower, upper):
+        low_part = jnp.maximum(lower - position, 0.0) / lower
+        high_part = jnp.maximum(upper - (count - 1.0 - position), 0.0) / upper
+        return low_part * low_part + high_part * high_part
+
+    row = lax.broadcasted_iota(jnp.int32, (ny, nz), 0)
+    column = lax.broadcasted_iota(jnp.int32, (ny, nz), 1)
+    flat = row * nz + column
+    BASE[...] = damp_peak * (
+        ramp_at(row.astype(jnp.float32), ny, edges[2], edges[3])
+        + ramp_at(column.astype(jnp.float32), nz, edges[4], edges[5])
+    )
+
+    @pl.loop(0, nx)
+    def _(i):
+        C[i] = coefficient(code_ref[i])
+        position = jnp.full((8, nz), (start_x + i).astype(jnp.float32))
+        along = ramp_at(position, 2 * nx, edges[0][0:8], edges[1][0:8])
+        A[i] = BASE[...] + damp_peak * jnp.concatenate([along] * (ny // 8), axis=0)
+
+    nothing = jnp.zeros((nx, 8, nz), jnp.float32)
+    for n in range(6):
+        fields[n][pl.ds(4, nx), 0:8, :] = nothing
+        fields[n][pl.ds(4, nx), ny + 8 : ny + 16, :] = nothing
+        fields[n][pl.ds((nx + 4) * core, 4), 8 : ny + 8, :] = jnp.zeros((4, ny, nz), jnp.float32)
+
+    def along_z(field, i):
+        v = field[pl.ds(i + 4, XB), 8 : ny + 8, :].reshape(XB * ny, nz)
+        high = v.astype(jnp.bfloat16)
+        low = (v - high.astype(jnp.float32)).astype(jnp.bfloat16)
+        both = jnp.dot(jnp.concatenate([high, low], axis=1), band_ref[...], preferred_element_type=jnp.float32)
+        return both[:, :nz] + both[:, nz:]
+
+    def plane_laplace(field, j, part):
+        v = field[j + 4, 8 : ny + 8, :]
+        total = 3.0 * STENCIL[0] * v + part
+        for k in range(1, 5):
+            total = total + STENCIL[k] * (
+                (field[j + 4 + k, 8 : ny + 8, :] + field[j + 4 - k, 8 : ny + 8, :])
+                + (field[j + 4, 8 + k : ny + 8 + k, :] + field[j + 4, 8 - k : ny + 8 - k, :])
+            )
+        return v, total
+
+    source = source_ref[0] - start_x * ny * nz
+
+    def wave_step(m):
+        halo(m).wait_recv()
+        amplitude = wavelet_ref[0, m]
+
+        @pl.loop(0, nx // XB)
+        def _(t):
+            part = along_z(fields[m], t * XB)
+            for p in range(XB):
+                j = t * XB + p
+                v, total = plane_laplace(fields[m], j, part[p * ny : (p + 1) * ny])
+                drive = C[j] * total
+                D[m, j] = drive
+                if m < 3:
+                    prior = prev_ref[j] if m == 0 else fields[m - 1][j + 4, 8 : ny + 8, :]
+                    change = v - prior
+                    later = v + change + drive - A[j] * change
+                    here = flat == source - j * (ny * nz)
+                    later = later + jnp.where(here, C[j] * amplitude, 0.0)
+                    fields[m + 1][j + 4, 8 : ny + 8, :] = later
+
+        if m < 3:
+            halo(m + 1).start()
+
+    def pack(dest, i, value):
+        tiles = swap_groups([value[8 * g : 8 * g + 8] for g in range(groups)], width)
+        for g in range(groups):
+            dest[g, i] = tiles[g]
+
+    def unpack(n, born, drive):
+        @pl.loop(0, nx)
+        def _(i):
+            tiles = swap_groups([G[n, g, i] for g in range(groups)], width)
+            model = jnp.concatenate(tiles, axis=0)
+            M[i] = model
+            fields[born][i + 4, 8 : ny + 8, :] = model * D[drive, i]
+
+        halo(born).start()
+
+    def born_step(born, drive, finish):
+        @pl.loop(0, nx // XB)
+        def _(t):
+            part = along_z(fields[born], t * XB)
+            for p in range(XB):
+                j = t * XB + p
+                v, total = plane_laplace(fields[born], j, part[p * ny : (p + 1) * ny])
+                later = 2.0 * v + C[j] * total - A[j] * v + M[j] * D[drive, j]
+                finish(j, v, later)
+
+    wave_step(0)
+    gather_forward(0, 1)
+    wave_step(1)
+    gather_forward(0, 2)
+
+    @pl.loop(0, nx)
+    def _(i):
+        pack(LP, i, D[0, i] * D[0, i] + D[1, i] * D[1, i])
+
+    gather_forward(0, 3)
+    pair_start(0)
+    H[...] = jnp.dot(
+        cos_ref[...], gain_ref[...], precision=lax.Precision.HIGHEST, preferred_element_type=jnp.float32
+    )
+    gather_end(0)
+    unpack(0, 4, 0)
+    halo(4).wait_recv()
+
+    def finish_image(j, v, later):
+        pack(IP, j, D[0, j] * v + D[1, j] * later)
+
+    born_step(4, 1, finish_image)
+    pair_start(1)
+    wave_step(2)
+    sum_line(0)
+    wave_step(3)
+    sum_line(1)
+    sum_own(0)
+    sum_own(1)
+
+    sub = lax.broadcasted_iota(jnp.int32, (8, nz), 0)
+
+    @pl.loop(0, nx // 2)
+    def _(t):
+        for p in range(2):
+            i = 2 * t + p
+            scaled = IP[shot, i] / (LP[shot, i] + eps)
+            moved = [scaled]
+            for q in range(1, 8):
+                turned = pltpu.roll(scaled, q, 0)
+                moved.append(jnp.where(sub < q, pltpu.roll(turned, width, 1), turned))
+            result = None
+            for g in range(groups):
+                term = moved[0] * H[8 * g : 8 * g + 1, :]
+                for q in range(1, 8):
+                    term = term + moved[q] * H[8 * g + q : 8 * g + q + 1, :]
+                if g:
+                    result = result + pltpu.roll(term, width * g, 1)
+                else:
+                    result = term
+            G[1, shot, i] = result
+
+    gather_start(1)
+
+    @pl.loop(0, nx)
+    def _(i):
+        tile = G[1, shot, i]
+        filt_ref[i, 0:8, :] = tile[:, 0:width]
+        for g in range(1, groups):
+            filt_ref[i, 8 * g : 8 * g + 8, :] = pltpu.roll(tile, nz - width * g, 1)[:, 0:width]
+
+    for d in (1, 2, 3):
+        gather_forward(1, d)
+    gather_end(1)
+    unpack(1, 5, 2)
+
+    count = receiver_ref.shape[1]
+    lanes = lax.broadcasted_iota(jnp.int32, (1, nz), 1)
+    ones = jnp.ones((8, nz), jnp.float32)
+
+    def record(m, read):
+        @pl.loop(0, count // 8)
+        def _(t):
+            for p in range(8):
+                r = t * 8 + p
+                local = receiver_ref[0, r] - start_x * ny * nz
+                owned = (local >= 0) & (local < nx * ny * nz)
+                safe = jnp.clip(local, 0, nx * ny * nz - 1)
+                at = jnp.where(owned, safe & (nz - 1), -1)
+                line = read(safe // (ny * nz), (safe // nz) & (ny - 1))
+                ROWS[pl.ds(r, 1), :] = jnp.where(lanes == at, line, 0.0)
+
+        TR[0, m] = lax.dot_general(
+            ones, ROWS[...], (((1,), (1,)), ((), ())),
+            precision=lax.Precision.HIGHEST, preferred_element_type=jnp.float32,
+        )
+
+    halo(5).wait_recv()
+    record(0, lambda px, py: B[1, px + 4, pl.ds(py + 8, 1), :])
+
+    def finish_born(j, v, later):
+        born_ref[j] = later
+
+    born_step(5, 3, finish_born)
+    record(1, lambda px, py: born_ref[px, pl.ds(py, 1), :])
+    swap = copy(TR.at[0], TR.at[1], tr_send, tr_recv, other)
+    swap.start()
+    for n in range(2):
+        gather_drain(n)
+        sum_drain(n)
+    for n in range(6):
+        halo(n).wait_send()
+    swap.wait()
+    for m in range(2):
+        trace_ref[m : m + 1, :] = TR[0, m, 0:1, :] + TR[1, m, 0:1, :]
+
+
+def fast_body(
+    wave_prev, wave_now, velocity_code, perturb, gains, wavelet, source_index, receiver_index, absorb_width
+):
+    shape = wave_now.shape[1:]
+    nx, ny, nz = shape
+    planes, receivers = gains.shape[0], receiver_index.shape[1]
+    groups = nz // planes
+    index = np.arange(ny)
+    cosine = (np.cos(2.0 * np.pi / ny * (index[:, None] * index[None, :] % ny)) / ny).astype(np.float32)
+    band = np.zeros((nz, nz), np.float32)
+    for k in range(1, 5):
+        band += STENCIL[k] * (np.eye(nz, k=k) + np.eye(nz, k=-k)).astype(np.float32)
+    high = band.astype(ml_dtypes.bfloat16)
+    low = (band - high.astype(np.float32)).astype(ml_dtypes.bfloat16)
+    band = np.concatenate([np.concatenate([high, low], 1)] * 2, 0)
+    tiled = jnp.tile(gains.T, (1, groups))
+    block = (nx, 8, nz)
+    f32 = jnp.float32
+    vmem = pl.BlockSpec(memory_space=pltpu.VMEM)
+    smem = pl.BlockSpec(memory_space=pltpu.SMEM)
+    v = lambda *dims: pltpu.VMEM(dims, f32)
+    dma = pltpu.SemaphoreType.DMA
+    filtered, born, traces = pl.pallas_call(
+        window_kernel,
+        out_shape=(
+            jax.ShapeDtypeStruct((nx, ny, planes), f32),
+            jax.ShapeDtypeStruct(shape, f32),
+            jax.ShapeDtypeStruct((STEPS_B, receivers), f32),
+        ),
+        in_specs=[vmem, pl.BlockSpec(memory_space=pl.ANY)] + [vmem] * 5 + [smem] * 4,
+        out_specs=(vmem, vmem, vmem),
+        scratch_shapes=[
+            v(4, nx + 8, ny + 16, nz),
+            v(4, *shape),
+            v(2, nx + 8, ny + 16, nz),
+            v(*shape),
+            v(*shape),
+            v(*shape),
+            v(ny, nz),
+            v(ny, nz),
+            v(2, groups, *block),
+        ]
+        + [v(groups, *block), v(4, *block), v(4, *block), v(4, *block)] * 2
+        + [
+            v(ny, nz),
+            v(receivers, nz),
+            v(2, STEPS_B, 8, receivers),
+            dma,
+            dma((6,)),
+            dma((6,)),
+            dma,
+            dma,
+            dma((2, 3, 4)),
+            dma((2, groups)),
+            dma((2, 3, 4)),
+            dma((2, 3, 4)),
+        ],
+        compiler_params=pltpu.CompilerParams(
+            collective_id=0, has_side_effects=True, vmem_limit_bytes=48 * 1024 * 1024
+        ),
+    )(
+        wave_prev.reshape(shape), wave_now.reshape(shape), velocity_code, perturb, tiled, cosine, band,
+        wavelet, source_index, receiver_index, absorb_width,
+    )
+    return filtered, born[None], traces[None]
+
+
+def choose(*args):
+    wave_now, gains = args[1], args[4]
+    shots, _, span_y, span_z = wave_now.shape
+    size = lax.axis_size("shot")
+    fits = shots == 1 and size == 8 and lax.axis_size("space") == 2
+    if fits and span_y == 64 and span_z == 128 and gains.shape[0] == 16:
+        return fast_body(*args)
+    return body(*args)
+
+
 def solution(mesh):
     in_specs = (
         P(("dom", "shot"), "space", None, None),
@@ -197,4 +711,4 @@
         P(("dom", "shot"), "space", None, None),
         P(("dom", "shot"), None, None),
     )
-    return jax.shard_map(body, mesh=mesh, in_specs=in_specs, out_specs=out_specs, check_vma=False)
+    return jax.shard_map(choose, mesh=mesh, in_specs=in_specs, out_specs=out_specs, check_vma=False)

time: 279 us -> 108 us (0.39)
  Pallas kernels: 0 us -> 98.4 us
  other arithmetic: 95.6 us -> 0 us
  waiting for transfers between devices: 73.2 us -> 0 us
  blocking collectives: 36.1 us -> 0 us
  between operations: 23.6 us -> 1.46 us
  local copies, waits for them, and re-layouts: 29.2 us -> 8.18 us
  starting transfers between devices: 13.6 us -> 0 us
  matrix products: 6.7 us -> 0 us
    pallas_call x0 -> x1, Pallas kernels: none -> 98.4 us  [fast_body(): pl.pallas_call(window_kernel, out_shape=(jax.ShapeDtypeStruct((nx, ny, pl...]
    add x10 -> x0, other arithmetic: 51.5 us -> none  [the longest x1 35.2 us: advance(): 2.0 * born + speed_term * laplace(born_padded) - absorber * born]
    psum x1 -> x0, waiting for transfers between devices: 41.5 us -> none  [body(): image_all, light_all = lax.psum((image, light), 'shot')]
    all_gather x1 -> x0, blocking collectives: 31.3 us -> none  [body(): table_all = lax.all_gather(gains, 'shot', axis=0, tiled=True)]
    all_gather x1 -> x0, waiting for transfers between devices: 29.7 us -> none  [body(): model = lax.all_gather(perturb, 'shot', axis=2, tiled=True)]
    sub x3 -> x0, other arithmetic: 26.4 us -> none  [advance(): 2.0 * current - prior + drive - absorber * (current - prior)]
    ppermute x8 -> x0, starting transfers between devices: 13.6 us -> none  [the longest x4 8.22 us: with_halo(): before = lax.ppermute(last, axis, up)]
    concatenate x4 -> x0, other arithmetic: 12.2 us -> none  [with_halo(): x = jnp.concatenate([before, x, after], axis=dim)]
  transfers between devices with their start and end apart: 10 -> 0, of which waited for: 3 -> 0; matrix products, arithmetic and copies ran while one was open for 16% -> 0% of each run, Pallas kernels for 0% -> 0%
where the time goes in v1:
time: 108 us
  Pallas kernels  98.4 us (91%)
  local copies, waits for them, and re-layouts  8.18 us (8%)
  between operations  1.46 us (1%)
    pallas_call x1, Pallas kernels, fast_body(): pl.pallas_call(window_kernel, out_shape=(jax.ShapeDtypeStruct((nx, ny, pl...  98.4 us
    unnamed x20, local copies, waits for them, and re-layouts  7.42 us

profile of v1, /device:TPU:0, one launch (start us, length us, event | category | flops | bytes accessed | tf_op | source)
XLA Modules:
  0.0 108.1 jit_solution(17115564570954883242)
XLA Ops:
  0.6 0.0 copy-start
  1.4 0.7 tile.4
  2.1 0.1 copy.18.gain_ref
  2.1 0.0 copy-start.3
  2.2 0.0 copy-start.4
  2.2 0.0 copy-start.5
  2.2 0.0 copy-start.6
  2.2 0.0 copy-start.7
  2.2 2.4 %copy.17.pert_ref = f32[32,64,16]{2,1,0:T(8,128)} copy(f32[32,64,16]{1,2,0:T(8,128)} %param.14) | data formatting | bytes 262144 | tf_op args[3]
  4.6 0.0 copy-done
  4.6 0.0 copy-done.3
  4.6 0.0 copy-done.4
  4.6 0.0 copy-done.5
  4.6 0.0 copy-done.6
  4.6 0.0 copy-done.7
  4.6 0.0 copy-start.1
  4.6 1.2 %copy-done.1 = f32[1,32,64,128]{3,2,1,0:T(8,128)S(1)} copy-done((f32[1,32,64,128]{3,2,1,0:T(8,128)S(1)}, f32[1,32,64,128]{3,2,1,0:T(8,128)}, u32[]{:S(2)}) %copy-start.1) | copy-done | bytes 1048600
  5.8 0.0 copy-start.2
  5.8 1.2 %copy-done.2 = s32[32,64,128]{2,1,0:T(8,128)S(1)} copy-done((s32[32,64,128]{2,1,0:T(8,128)S(1)}, s32[32,64,128]{2,1,0:T(8,128)}, u32[]{:S(2)}) %copy-start.2) | copy-done | bytes 1048600
  7.1 98.4 %shard_map.130 = (f32[32,64,16]{2,1,0:T(8,128)S(1)}, f32[32,64,128]{2,1,0:T(8,128)S(1)}, f32[2,256]{1,0:T(2,128)S(1)}) custom-call(f32[32,64,128]{2,1,0:T(8,128)S(1)} %bitcast.7, f32[32,64,128]{2,1,0:T(8,128)S(1)} %bitcast.8, s32[32,64,128]{2,1,0:T(8,128)S(1)} %copy-done.2, f32[32,64,16]{2,1,0:T(8,128)} %copy.17.pert_ref, f32[64,128]{1,0:T(8,128)S(1)} %copy.18.gain_ref, ...), custom_call_target="tpu_custom_call" | custom-call | tf_op jit(solution)/shard_map/pallas_call | solution.py:642
  105.5 1.0 copy.19
  106.5 1.0 copy.23
  107.5 0.6 copy.24
Async XLA Ops:
  0.6 3.9 %copy-start = (f32[1,32,64,128]{3,2,1,0:T(8,128)S(1)}, f32[1,32,64,128]{3,2,1,0:T(8,128)}, u32[]{:S(2)}) copy-start(f32[1,32,64,128]{3,2,1,0:T(8,128)} %param.11) | copy-start | bytes 3145732
  2.1 2.4 %copy-start.3 = (bf16[256,256]{1,0:T(8,128)(2,1)S(1)}, bf16[256,256]{1,0:T(8,128)(2,1)}, u32[]{:S(2)}) copy-start(bf16[256,256]{1,0:T(8,128)(2,1)} %constant.5.clone.band_ref) | copy-start | bytes 393220
  2.2 2.4 %copy-start.4 = (f32[64,64]{1,0:T(8,128)S(1)}, f32[64,64]{1,0:T(8,128)}, u32[]{:S(2)}) copy-start(f32[64,64]{1,0:T(8,128)} %constant.4.clone.cos_ref) | copy-start | bytes 49156
  2.2 2.4 %copy-start.5 = (s32[1,256]{1,0:T(1,128)S(1)}, s32[1,256]{1,0:T(1,128)}, u32[]{:S(2)}) copy-start(s32[1,256]{1,0:T(1,128)} %receiver_ref.1) | copy-start | bytes 3076
  2.2 2.4 %copy-start.6 = (f32[1,4]{1,0:T(1,128)S(1)}, f32[1,4]{1,0:T(1,128)}, u32[]{:S(2)}) copy-start(f32[1,4]{1,0:T(1,128)} %wavelet_ref.1) | copy-start | bytes 52
  2.2 2.4 %copy-start.7 = (s32[6]{0:T(128)S(1)}, s32[6]{0:T(128)}, u32[]{:S(2)}) copy-start(s32[6]{0:T(128)} %width_ref.1) | copy-start | bytes 76
  4.6 1.2 %copy-start.1 = (f32[1,32,64,128]{3,2,1,0:T(8,128)S(1)}, f32[1,32,64,128]{3,2,1,0:T(8,128)}, u32[]{:S(2)}) copy-start(f32[1,32,64,128]{3,2,1,0:T(8,128)} %param.12) | copy-start | bytes 3145732
  5.8 1.2 %copy-start.2 = (s32[32,64,128]{2,1,0:T(8,128)S(1)}, s32[32,64,128]{2,1,0:T(8,128)}, u32[]{:S(2)}) copy-start(s32[32,64,128]{2,1,0:T(8,128)} %code_ref.1) | copy-start | bytes 3145732

commit v2 on v1

--- a/solution.py
+++ b/solution.py
@@ -207,16 +207,16 @@
     prev_ref, now_ref, code_ref, pert_ref, gain_ref, cos_ref, band_ref,
     wavelet_ref, source_ref, receiver_ref, width_ref,
     filt_ref, born_ref, trace_ref,
-    W, D, B, M, C, A, PAD, BASE, G, LP, LY, LU, LD, IP, IY, IU, ID, H, ROWS, TR,
-    in_sem, halo_send, halo_recv, tr_send, tr_recv,
+    W, D, B, M, C, A, CODE, PREV, BASE, G, LP, LY, LU, LD, IP, IY, IU, ID, H, ROWS, TR,
+    in_sem, code_sem, prev_sem, halo_send, halo_recv, tr_send, tr_recv,
     g_send, g_recv, rs_send, rs_recv,
 ):
     core = lax.axis_index("space")
     shot = lax.axis_index("shot")
     y = lax.rem(shot, 2)
     z = shot // 2
-    nx, ny, nz = code_ref.shape
-    width = pert_ref.shape[2]
+    nx, ny, nz = C.shape
+    width = pert_ref.shape[1]
     groups = nz // width
     start_x = core * nx
     other = {"space": 1 - core}
@@ -226,6 +226,10 @@
 
     load = pltpu.make_async_copy(now_ref, W.at[0, pl.ds(4, nx), pl.ds(8, ny)], in_sem)
     load.start()
+    load_code = pltpu.make_async_copy(code_ref, CODE, code_sem)
+    load_code.start()
+    load_prev = pltpu.make_async_copy(prev_ref, PREV, prev_sem)
+    load_prev.start()
 
     barrier = pltpu.get_barrier_semaphore()
     pl.semaphore_signal(barrier, inc=1, device_id=other, device_id_type=MESH)
@@ -239,15 +243,11 @@
     def _():
         pl.semaphore_signal(barrier, inc=1, device_id=below, device_id_type=MESH)
 
-    lane_group = lax.broadcasted_iota(jnp.int32, (8, nz), 1) // width
-
-    @pl.loop(0, nx)
-    def _(i):
-        PAD[:, 0:width] = pert_ref[i]
-        tile = PAD[0:8, :]
-        for g in range(1, groups):
-            tile = jnp.where(lane_group == g, pltpu.roll(PAD[8 * g : 8 * g + 8, :], width * g, 1), tile)
-        G[0, shot, i] = tile
+    for t in range(nx // groups):
+        turned = pert_ref[groups * t : groups * t + groups].reshape(nz, ny).T
+        tiles = swap_groups([turned[8 * g : 8 * g + 8] for g in range(groups)], width)
+        for g in range(groups):
+            G[0, shot, groups * t + g] = tiles[g]
 
     @pl.when((z > 0) & (z < 3))
     def _():
@@ -430,9 +430,11 @@
         + ramp_at(column.astype(jnp.float32), nz, edges[4], edges[5])
     )
 
+    load_code.wait()
+
     @pl.loop(0, nx)
     def _(i):
-        C[i] = coefficient(code_ref[i])
+        C[i] = coefficient(CODE[i])
         position = jnp.full((8, nz), (start_x + i).astype(jnp.float32))
         along = ramp_at(position, 2 * nx, edges[0][0:8], edges[1][0:8])
         A[i] = BASE[...] + damp_peak * jnp.concatenate([along] * (ny // 8), axis=0)
@@ -475,7 +477,7 @@
                 drive = C[j] * total
                 D[m, j] = drive
                 if m < 3:
-                    prior = prev_ref[j] if m == 0 else fields[m - 1][j + 4, 8 : ny + 8, :]
+                    prior = PREV[j] if m == 0 else fields[m - 1][j + 4, 8 : ny + 8, :]
                     change = v - prior
                     later = v + change + drive - A[j] * change
                     here = flat == source - j * (ny * nz)
@@ -510,20 +512,22 @@
                 later = 2.0 * v + C[j] * total - A[j] * v + M[j] * D[drive, j]
                 finish(j, v, later)
 
+    gather_forward(0, 1)
+    load_prev.wait()
     wave_step(0)
-    gather_forward(0, 1)
+    gather_forward(0, 2)
     wave_step(1)
-    gather_forward(0, 2)
+    gather_forward(0, 3)
 
     @pl.loop(0, nx)
     def _(i):
         pack(LP, i, D[0, i] * D[0, i] + D[1, i] * D[1, i])
 
-    gather_forward(0, 3)
     pair_start(0)
     H[...] = jnp.dot(
         cos_ref[...], gain_ref[...], precision=lax.Precision.HIGHEST, preferred_element_type=jnp.float32
     )
+    wave_step(2)
     gather_end(0)
     unpack(0, 4, 0)
     halo(4).wait_recv()
@@ -533,7 +537,6 @@
 
     born_step(4, 1, finish_image)
     pair_start(1)
-    wave_step(2)
     sum_line(0)
     wave_step(3)
     sum_line(1)
@@ -564,12 +567,10 @@
 
     gather_start(1)
 
-    @pl.loop(0, nx)
-    def _(i):
-        tile = G[1, shot, i]
-        filt_ref[i, 0:8, :] = tile[:, 0:width]
-        for g in range(1, groups):
-            filt_ref[i, 8 * g : 8 * g + 8, :] = pltpu.roll(tile, nz - width * g, 1)[:, 0:width]
+    for t in range(nx // groups):
+        tiles = swap_groups([G[1, shot, groups * t + g] for g in range(groups)], width)
+        turned = jnp.concatenate(tiles, axis=0).T
+        filt_ref[groups * t : groups * t + groups] = turned.reshape(groups, width, ny)
 
     for d in (1, 2, 3):
         gather_forward(1, d)
@@ -642,11 +643,11 @@
     filtered, born, traces = pl.pallas_call(
         window_kernel,
         out_shape=(
-            jax.ShapeDtypeStruct((nx, ny, planes), f32),
+            jax.ShapeDtypeStruct((nx, planes, ny), f32),
             jax.ShapeDtypeStruct(shape, f32),
             jax.ShapeDtypeStruct((STEPS_B, receivers), f32),
         ),
-        in_specs=[vmem, pl.BlockSpec(memory_space=pl.ANY)] + [vmem] * 5 + [smem] * 4,
+        in_specs=[pl.BlockSpec(memory_space=pl.ANY)] * 3 + [vmem] * 4 + [smem] * 4,
         out_specs=(vmem, vmem, vmem),
         scratch_shapes=[
             v(4, nx + 8, ny + 16, nz),
@@ -655,7 +656,8 @@
             v(*shape),
             v(*shape),
             v(*shape),
-            v(ny, nz),
+            pltpu.VMEM(shape, jnp.int32),
+            v(*shape),
             v(ny, nz),
             v(2, groups, *block),
         ]
@@ -664,6 +666,8 @@
             v(ny, nz),
             v(receivers, nz),
             v(2, STEPS_B, 8, receivers),
+            dma,
+            dma,
             dma,
             dma((6,)),
             dma((6,)),
@@ -675,13 +679,13 @@
             dma((2, 3, 4)),
         ],
         compiler_params=pltpu.CompilerParams(
-            collective_id=0, has_side_effects=True, vmem_limit_bytes=48 * 1024 * 1024
+            collective_id=0, has_side_effects=True, vmem_limit_bytes=60 * 1024 * 1024
         ),
     )(
-        wave_prev.reshape(shape), wave_now.reshape(shape), velocity_code, perturb, tiled, cosine, band,
+        wave_prev.reshape(shape), wave_now.reshape(shape), velocity_code, perturb.transpose(0, 2, 1), tiled, cosine, band,
         wavelet, source_index, receiver_index, absorb_width,
     )
-    return filtered, born[None], traces[None]
+    return filtered.transpose(0, 2, 1), born[None], traces[None]
 
 
 def choose(*args):

time: 108 us -> 104 us (0.963)
  local copies, waits for them, and re-layouts: 8.18 us -> 5.29 us
  Pallas kernels: 98.4 us -> 97.3 us
    unnamed x20 -> x7, local copies, waits for them, and re-layouts: 7.42 us -> 4.59 us
    pallas_call x1, Pallas kernels: 98.4 us -> 97.3 us  [fast_body(): pl.pallas_call(window_kernel, out_shape=(jax.ShapeDtypeStruct((nx, planes...]
where the time goes in v2:
time: 104 us
  Pallas kernels  97.3 us (94%)
  local copies, waits for them, and re-layouts  5.29 us (5%)
  between operations  1.31 us (1%)
    pallas_call x1, Pallas kernels, fast_body(): pl.pallas_call(window_kernel, out_shape=(jax.ShapeDtypeStruct((nx, planes...  97.3 us
    unnamed x7, local copies, waits for them, and re-layouts  4.59 us

profile of v2, /device:TPU:0, one launch (start us, length us, event | category | flops | bytes accessed | tf_op | source)
XLA Modules:
  0.0 103.9 jit_solution(16009834776727211125)
XLA Ops:
  0.6 0.0 copy-start
  1.3 0.0 copy-done
  1.3 0.7 copy.15.gain_ref
  2.0 97.3 %shard_map.130 = (f32[32,16,64]{2,1,0:T(8,128)}, f32[32,64,128]{2,1,0:T(8,128)}, f32[2,256]{1,0:T(2,128)}) custom-call(f32[32,64,128]{2,1,0:T(8,128)} %bitcast.8, f32[32,64,128]{2,1,0:T(8,128)} %bitcast.9, s32[32,64,128]{2,1,0:T(8,128)} %code_ref.1, f32[32,16,64]{2,1,0:T(8,128)} %bitcast.11, f32[64,128]{1,0:T(8,128)} %copy.15.gain_ref, ...), custom_call_target="tpu_custom_call" | custom-call | tf_op jit(solution)/shard_map/pallas_call | solution.py:643
  99.3 1.7 %copy.20 = f32[32,64,16]{1,2,0:T(8,128)} copy(f32[32,64,16]{1,2,0:T(8,128)} %bitcast.13) | data formatting | bytes 262144
  101.0 0.0 copy-start.1
  101.0 2.3 %copy.21 = f32[1,32,64,128]{3,2,1,0:T(8,128)} copy(f32[1,32,64,128]{3,2,1,0:T(8,128)} %bitcast.10) | data formatting | bytes 2097152
  103.3 0.0 copy-done.1
  103.3 0.6 copy.22
  (1 shorter events, 0.0 us)
Async XLA Ops:
  0.6 0.7 copy-start
  101.0 2.3 %copy-start.1 = (f32[2,256]{1,0:T(2,128)S(1)}, f32[2,256]{1,0:T(2,128)}, u32[]{:S(2)}) copy-start(f32[2,256]{1,0:T(2,128)} %get-tuple-element.8) | copy-start | bytes 6148
